TPU v7x, 1024 devices: a whole 8x8x8 slice. The times are simulated.
1024 devices in a mesh: dp: 64 (over x, z), expert: 16 (over y, core).
Axes of the slice: x: 8, y: 8, z: 8, core: 2. Of those that a mesh axis runs over, the one named last changes fastest.
Arguments:
- d_out: bfloat16 [131072, 5120], P(('dp', 'expert')), may hold values from -6 to 6
- routes: int32 [131072, 1], P(('dp', 'expert')), may hold values from 0 to 15; in each aligned block of 128 rows (0 to 127, 128 to 255, ...) at most 10 rows name the same one
- gates: bfloat16 [131072, 1], P(('dp', 'expert')), may hold values from 0.01 to 1, as said below
- slot_hidden: bfloat16 [64, 16, 16, 10, 768], P('dp', None, 'expert'), may hold values from -0.59765625 to 0.59765625
- w_down: bfloat16 [16, 768, 5120], P('expert'), may hold values from -0.078125 to 0.078125
- balance_coef: float32 [], replicated, may hold values from 0.5 to 2
Outputs:
- d_probs: float32 [131072, 16], P(('dp', 'expert'))
- d_hidden: bfloat16 [64, 16, 16, 10, 768], P('dp', None, 'expert')
Inputs may be any that keep to these rules, and one draw needn't show every extreme that they name: `routes`: within each aligned block of 128 rows (the rows of one device) no expert is named by more than 10 pairs, a bound that some block reaches. `gates`: positive gate weights.
All inputs are finite; a program needn't handle non-finite values.
Results may differ from a plain program's by a relative error of at most 0.007.
Values may be sent and summed in bfloat16 or wider, within the bound.
No kernel may reach another device: no remote copies, remote signals or barrier semaphores. Data moves between devices by JAX's collectives and lax.ppermute only.
A program may use at most 64 MiB of HBM per device.

v0:
```python
import jax
import jax.numpy as jnp
from jax import lax
from jax.sharding import PartitionSpec as P


def on_device(d_out, routes, gates, slot_hidden, w_down, balance_coef):
    tok_rows = d_out.shape[0]
    width = d_out.shape[1]
    top_count = routes.shape[1]
    groups = lax.axis_size("expert")
    local_experts = w_down.shape[0]
    expert_count = groups * local_experts
    slots = slot_hidden.shape[3]
    hidden_units = slot_hidden.shape[4]
    flat = routes.reshape(-1)
    flat_gate = gates.reshape(-1)
    onehot = (flat[:, None] == jnp.arange(expert_count, dtype=jnp.int32)[None, :]).astype(jnp.int32)
    ranks = jnp.sum((jnp.cumsum(onehot, 0) - onehot) * onehot, 1)
    owner_rows = jnp.arange(tok_rows * top_count, dtype=jnp.int32) // top_count
    token_rows = d_out[owner_rows]
    send_rows = (
        jnp.zeros((expert_count, slots, width), jnp.bfloat16).at[flat, ranks].set(token_rows)
    )
    send_gate = jnp.zeros((expert_count, slots), jnp.bfloat16).at[flat, ranks].set(flat_gate)
    recv_rows, recv_gate = (
        lax.all_to_all(send_rows, "expert", split_axis=0, concat_axis=0, tiled=True),
        lax.all_to_all(send_gate, "expert", split_axis=0, concat_axis=0, tiled=True),
    )
    recv_rows = recv_rows.reshape(groups, local_experts, slots, width)
    recv_gate = recv_gate.reshape(groups, local_experts, slots).astype(jnp.float32)
    saved = slot_hidden.reshape(groups, local_experts, slots, hidden_units)
    y_out = jnp.einsum("secf,efd->secd", saved, w_down, preferred_element_type=jnp.float32).astype(
        jnp.bfloat16
    )
    dproj = jnp.einsum("secd,efd->secf", recv_rows, w_down, preferred_element_type=jnp.float32)
    d_hidden = (dproj * recv_gate[:, :, :, None]).astype(jnp.bfloat16)
    d_hidden = d_hidden.reshape(1, groups, local_experts, slots, hidden_units)
    back = lax.all_to_all(
        y_out.reshape(expert_count, slots, width), "expert", split_axis=0, concat_axis=0, tiled=True
    )
    picked = back[flat, ranks]
    pair_score = jnp.sum(token_rows.astype(jnp.float32) * picked.astype(jnp.float32), -1)
    local_mass = jnp.sum(onehot.astype(jnp.float32) * flat_gate.astype(jnp.float32)[:, None], 0)
    total_mass = lax.psum(local_mass, ("dp", "expert"))
    all_tokens = tok_rows * lax.axis_size("dp") * groups
    load = expert_count * total_mass / (top_count * all_tokens)
    routed = (onehot.astype(jnp.float32) * pair_score[:, None]).reshape(
        tok_rows, top_count, expert_count
    )
    d_probs = balance_coef * load[None, :] + jnp.sum(routed, 1)
    return (d_probs, d_hidden)


def solution(mesh):
    return jax.shard_map(
        on_device,
        mesh=mesh,
        in_specs=(
            P(("dp", "expert"), None),
            P(("dp", "expert"), None),
            P(("dp", "expert"), None),
            P("dp", None, "expert", None, None),
            P("expert", None, None),
            P(),
        ),
        out_specs=(P(("dp", "expert"), None), P("dp", None, "expert", None, None)),
        check_vma=False,
    )
```

profile of v0, /device:TPU:1, one launch (start us, length us, event | category | flops | bytes accessed | tf_op | source)
XLA Modules:
  0.0 300.1 jit_solution(6829874442882201045)
XLA Ops:
  0.6 0.0 copy-start
  0.6 0.8 fusion.13
  1.5 0.2 reduce_window_sum.11
  1.7 0.8 select_reduce_fusion
  2.5 0.7 fusion.15
  3.2 11.2 %scatter_fusion.1 = bf16[16,10]{1,0:T(8,128)(2,1)S(1)} fusion(bf16[16,10]{1,0:T(8,128)(2,1)S(1)} %broadcast_in_dim.5, s32[128]{0:T(128)S(1)} %get-tuple-element.6, bf16[128]{0:T(256)(128)(2,1)} %bitcast.54), kind=kCustom, calls=%fused_computation.3 | custom fusion | bytes 1792 | tf_op jit(solution)/shard_map/scatter | solution.py:25
  14.3 0.6 copy.14
  14.9 17.4 %all-to-all-start.2 = ((bf16[16,1,10]{2,1,0:T(2,128)(2,1)}), bf16[16,1,10]{2,1,0:T(2,128)(2,1)S(1)}, u32[]{:S(2)}, u32[]{:S(2)}) async-start(bf16[16,1,10]{2,1,0:T(2,128)(2,1)} %copy.14), calls=%async_computation.2 | async-start | bytes 16384 | tf_op jit(solution)/shard_map/all_to_all | solution.py:28
  32.4 4.7 %fusion.7 = bf16[16,10,5120]{2,0,1:T(8,128)(2,1)S(1)} fusion(bf16[1,768,5120]{2,1,0:T(8,128)(2,1)} %param.10, bf16[1,16,1,10,768]{4,1,3,2,0:T(8,128)(2,1)} %param.9), kind=kOutput, calls=%fused_computation.9 | convolution fusion | flops 1259110400 | bytes 9748480 | tf_op jit(solution)/shard_map/secf,efd->secd/dot_general | solution.py:33
  37.0 2.5 copy.10
  39.6 0.0 all-to-all-done.2
  39.6 7.3 %all-to-all-start = ((bf16[16,10,5120]{2,1,0:T(8,128)(2,1)}), bf16[16,10,5120]{2,1,0:T(8,128)(2,1)}, u32[]{:S(2)}, u32[]{:S(2)}) async-start(bf16[16,10,5120]{2,1,0:T(8,128)(2,1)} %copy.10), calls=%async_computation | async-start | bytes 5242880 | tf_op jit(solution)/shard_map/all_to_all | solution.py:39
  46.9 0.0 copy-done
  46.9 2.5 gather_fusion
  49.4 0.2 broadcast_in_dim.4
  49.5 30.2 %scatter_fusion = bf16[16,10,5120]{2,0,1:T(8,128)(2,1)S(1)} fusion(bf16[16,10,5120]{2,0,1:T(8,128)(2,1)S(1)} %broadcast_in_dim.4, s32[128]{0:T(128)S(1)} %get-tuple-element.6, bf16[128,5120]{1,0:T(8,128)(2,1)} %gather_fusion), kind=kCustom, calls=%fused_computation.2 | custom fusion | bytes 3933184 | tf_op jit(solution)/shard_map/scatter | solution.py:23
  79.8 2.5 copy.12
  82.3 0.0 copy-start.2
  82.3 0.0 copy-start.1
  82.3 24.5 %all-to-all-done = bf16[16,10,5120]{2,1,0:T(8,128)(2,1)} async-done(((bf16[16,10,5120]{2,1,0:T(8,128)(2,1)}), bf16[16,10,5120]{2,1,0:T(8,128)(2,1)}, u32[]{:S(2)}, u32[]{:S(2)}) %all-to-all-start) | async-done | bytes 1638432 | tf_op jit(solution)/shard_map/all_to_all | solution.py:39
  106.7 5.4 %all-to-all-start.1 = ((bf16[16,10,5120]{2,1,0:T(8,128)(2,1)}), bf16[16,10,5120]{2,1,0:T(8,128)(2,1)}, u32[]{:S(2)}, u32[]{:S(2)}) async-start(bf16[16,10,5120]{2,1,0:T(8,128)(2,1)} %copy.12), calls=%async_computation.1 | async-start | bytes 5242880 | tf_op jit(solution)/shard_map/all_to_all | solution.py:27
  112.1 0.0 copy-done.2
  112.1 0.0 copy-done.1
  112.2 0.1 multiply_reduce_fusion.1
  112.3 168.5 %psum.7 = f32[16]{0:T(128)S(1)} all-reduce(f32[16]{0:T(128)S(1)} %multiply_reduce_fusion.1), channel_id=1, replica_groups=mesh['dp'=64,'expert'=16] {'dp','expert'}, use_global_device_ids=true, to_apply=%region_1.2 | all-reduce | flops 16 | bytes 128 | tf_op jit(solution)/shard_map/psum | solution.py:45
  281.5 0.1 copy.15
  281.5 2.6 copy.11
  284.2 5.8 %gather_fusion.1 = bf16[128,5120]{1,0:T(8,128)(2,1)} fusion(bf16[16,10,5120]{2,0,1:T(8,128)(2,1)S(1)} %copy.11, s32[128]{0:T(128)S(1)} %bitcast.48), kind=kCustom, calls=%fused_computation.1 | custom fusion | bytes 2622464 | tf_op jit(solution)/shard_map/gather | solution.py:42
  289.9 2.2 multiply_reduce_fusion
  292.1 0.1 multiply_add_fusion
  292.2 0.7 copy.16
  292.9 0.0 all-to-all-done.1
  292.9 6.3 %fusion = f32[16,10,768]{2,1,0:T(8,128)S(1)} fusion(bf16[16,10,5120]{2,1,0:T(8,128)(2,1)} %all-to-all-done.1, bf16[1,768,5120]{2,1,0:T(8,128)(2,1)} %param.10), kind=kOutput, calls=%fused_computation.4 | convolution fusion | flops 1258291200 | bytes 9994240 | tf_op jit(solution)/shard_map/secd,efd->secf/dot_general | solution.py:36
  299.2 1.0 fusion.11
  (6 shorter events, 0.0 us)
Async XLA Ops:
  0.6 46.2 %copy-start = (bf16[128,5120]{1,0:T(8,128)(2,1)S(1)}, bf16[128,5120]{1,0:T(8,128)(2,1)}, u32[]{:S(2)}) copy-start(bf16[128,5120]{1,0:T(8,128)(2,1)} %param.6) | copy-start | bytes 3932164
  14.9 24.6 %all-to-all-start.2 = ((bf16[16,1,10]{2,1,0:T(2,128)(2,1)}), bf16[16,1,10]{2,1,0:T(2,128)(2,1)S(1)}, u32[]{:S(2)}, u32[]{:S(2)}) async-start(bf16[16,1,10]{2,1,0:T(2,128)(2,1)} %copy.14), calls=%async_computation.2 | async-start | bytes 16384 | tf_op jit(solution)/shard_map/all_to_all | solution.py:28
  39.6 67.2 %all-to-all-start = ((bf16[16,10,5120]{2,1,0:T(8,128)(2,1)}), bf16[16,10,5120]{2,1,0:T(8,128)(2,1)}, u32[]{:S(2)}, u32[]{:S(2)}) async-start(bf16[16,10,5120]{2,1,0:T(8,128)(2,1)} %copy.10), calls=%async_computation | async-start | bytes 5242880 | tf_op jit(solution)/shard_map/all_to_all | solution.py:39
  82.3 29.8 %copy-start.2 = (bf16[128,1]{0,1:T(2,128)(2,1)S(1)}, bf16[128,1]{0,1:T(2,128)(2,1)}, u32[]{:S(2)}) copy-start(bf16[128,1]{0,1:T(2,128)(2,1)} %param.8) | copy-start | bytes 772
  82.3 29.9 %copy-start.1 = (s32[128,1]{0,1:T(1,128)S(1)}, s32[128,1]{0,1:T(1,128)}, u32[]{:S(2)}) copy-start(s32[128,1]{0,1:T(1,128)} %param.7) | copy-start | bytes 1540
  106.7 186.1 %all-to-all-start.1 = ((bf16[16,10,5120]{2,1,0:T(8,128)(2,1)}), bf16[16,10,5120]{2,1,0:T(8,128)(2,1)}, u32[]{:S(2)}, u32[]{:S(2)}) async-start(bf16[16,10,5120]{2,1,0:T(8,128)(2,1)} %copy.12), calls=%async_computation.1 | async-start | bytes 5242880 | tf_op jit(solution)/shard_map/all_to_all | solution.py:27
where the time goes:
time: 301 us; the launch traced here: 300 us
  blocking collectives  169 us (56%)
  local copies, waits for them, and re-layouts  58.9 us (20%)
  starting transfers between devices  30.1 us (10%)
  waiting for transfers between devices  24.5 us (8%)
  matrix products  10.9 us (4%)
  other arithmetic  5.88 us (2%)
    psum x1, blocking collectives, on_device(): total_mass = lax.psum(local_mass, ('dp', 'expert'))  169 us
    scatter x2, local copies, waits for them, and re-layouts, on_device(): jnp.zeros((expert_count, slots, width), jnp.bfloat16).at[flat, ranks]  32.8 us
    all_to_all x1, waiting for transfers between devices, on_device(): lax.all_to_all(y_out.reshape(expert_count, slots, width), 'expert', split...  24.5 us
    all_to_all x1, starting transfers between devices, on_device(): lax.all_to_all(send_gate, 'expert', split_axis=0, concat_axis=0, tiled=True)  17.4 us
    scatter x1, local copies, waits for them, and re-layouts, on_device(): jnp.zeros((expert_count, slots), jnp.bfloat16).at[flat, ranks]  11.2 us
    all_to_all x1, starting transfers between devices, on_device(): lax.all_to_all(y_out.reshape(expert_count, slots, width), 'expert', split...  7.27 us
    dot_general x1, matrix products, on_device(): jnp.einsum('secd,efd->secf', recv_rows, w_down, preferred_element_type=jn...  6.26 us
  transfers between devices with their start and end apart: 3, of which 1 were waited for; matrix products, arithmetic and copies ran while one was open for 18% of the time, Pallas kernels for 0%

commit v1 on v0

v1 whole, which is shorter than its diff:
```python
import functools

import jax
import jax.numpy as jnp
from jax import lax
from jax.experimental import pallas as pl
from jax.experimental.pallas import tpu as pltpu
from jax.sharding import PartitionSpec as P

F32 = jnp.float32
BF16 = jnp.bfloat16
SUB = 8


def iota(shape, axis):
    return lax.broadcasted_iota(jnp.int32, shape, axis)


def pack_kernel(blocks, routes_ref, gates_ref, rows_ref, send_ref, rank_ref, mass_ref):
    tokens, width = rows_ref.shape
    out_rows = send_ref.shape[0]
    experts = out_rows // SUB
    part = width // blocks
    routes = routes_ref[...]
    gates = gates_ref[...].astype(F32)
    onehot = (iota((experts, tokens), 0) == routes).astype(F32)
    earlier = (iota((tokens, tokens), 0) < iota((tokens, tokens), 1)).astype(BF16)
    before = jnp.dot(onehot.astype(BF16), earlier, preferred_element_type=F32)
    rank = jnp.sum(before * onehot, axis=0, keepdims=True).astype(jnp.int32)
    rank_ref[...] = rank
    mass = jnp.sum(onehot * gates, axis=1, keepdims=True)
    lane = iota((SUB, mass_ref.shape[1]), 1)
    total = jnp.zeros(mass_ref.shape, F32)
    for half in range(experts // SUB):
        total += jnp.where(lane == 2 + half, mass[half * SUB : (half + 1) * SUB], 0.0)
    mass_ref[...] = total
    row = iota((out_rows, tokens), 0)
    first = jnp.where(rank < SUB, routes * SUB + rank, -1)
    pick = jnp.where(row == first, gates, 0.0).astype(BF16)
    send_ref[:, :width] = jnp.dot(pick, rows_ref[...], preferred_element_type=F32).astype(BF16)
    late = jnp.where(rank >= SUB, routes * SUB + (rank - SUB) * blocks, -out_rows)
    tail = jnp.zeros((out_rows, part), F32)
    for b in range(blocks):
        pick = jnp.where(row == late + b, gates, 0.0).astype(BF16)
        tail += jnp.dot(pick, rows_ref[:, b * part : (b + 1) * part], preferred_element_type=F32)
    send_ref[:, width:] = tail.astype(BF16)


def hidden_kernel(blocks, slots, recv_ref, w_ref, hid_ref, mass_ref, dhid_ref, ret_ref, x_ref, score_ref):
    rows = recv_ref.shape[0]
    width = x_ref.shape[1]
    part = width // blocks
    groups = rows // SUB
    late = slots - SUB
    step = pl.program_id(0)

    @pl.when(step == 0)
    def _():
        x_ref[:rows, :] = recv_ref[:, :width]
        block = iota((rows, part), 0) % blocks
        tail = recv_ref[:, width:]
        for b in range(blocks):
            x_ref[rows:, b * part : (b + 1) * part] = jnp.where(block == b, tail, jnp.zeros_like(tail))
        score_ref[...] = jnp.zeros_like(score_ref)

    proj = lax.dot_general(
        x_ref[...], w_ref[...], (((1,), (1,)), ((), ())), preferred_element_type=F32
    )
    units = proj.shape[1]
    r = iota((rows, slots * groups), 0)
    q = iota((rows, slots * groups), 1)
    hid = hid_ref[...]
    pick_main = ((q // groups == r % SUB) & (q % groups == r // SUB)).astype(BF16)
    pick_late = ((q // groups == SUB + (r % SUB) // blocks) & (q % groups == r // SUB)).astype(BF16)
    main_hid = jnp.dot(pick_main, hid, preferred_element_type=F32)
    late_hid = jnp.dot(pick_late, hid, preferred_element_type=F32)
    main = jnp.sum(main_hid * proj[:rows], axis=1, keepdims=True)
    rest = jnp.sum(late_hid * proj[rows:], axis=1, keepdims=True)
    lane = iota(score_ref.shape, 1)
    score_ref[...] += jnp.where(lane == 0, main, 0.0) + jnp.where(lane == 1, rest, 0.0)
    late_proj = jnp.sum(proj[rows:].reshape(groups * late, blocks, units), axis=1)
    o = iota((slots * groups, rows), 0)
    i = iota((slots * groups, rows), 1)
    put_main = ((o // groups == i % SUB) & (o % groups == i // SUB)).astype(BF16)
    o = iota((slots * groups, groups * late), 0)
    i = iota((slots * groups, groups * late), 1)
    put_late = ((o // groups == SUB + i % late) & (o % groups == i // late)).astype(BF16)
    out = jnp.dot(put_main, proj[:rows].astype(BF16), preferred_element_type=F32)
    out += jnp.dot(put_late, late_proj.astype(BF16), preferred_element_type=F32)
    dhid_ref[...] = out.astype(BF16)

    @pl.when(step == pl.num_programs(0) - 1)
    def _():
        mass = jnp.broadcast_to(mass_ref[...][None], (groups, SUB, mass_ref.shape[1]))
        ret_ref[...] = score_ref[...] + mass.reshape(score_ref.shape)


def probs_kernel(blocks, scale, coef_ref, routes_ref, gates_ref, rank_ref, back_ref, out_ref):
    experts, tokens = out_ref.shape
    rows = back_ref.shape[0]
    routes = routes_ref[...]
    rank = rank_ref[...]
    gates = gates_ref[...].astype(F32)
    back = back_ref[...]
    row = iota((rows, tokens), 0)
    first = jnp.where(rank < SUB, routes * SUB + rank, -1)
    late = jnp.where(rank >= SUB, routes * (SUB // blocks) + (rank - SUB), -1)
    hits = jnp.where(row == first, back[:, 0:1], 0.0)
    hits += jnp.where(row // blocks == late, back[:, 1:2], 0.0)
    score = jnp.sum(hits, axis=0, keepdims=True) / gates
    mass = jnp.sum(back.reshape(rows // SUB, SUB, back.shape[1]), axis=0)
    coef = coef_ref[0, 0] * scale
    for half in range(experts // SUB):
        expert = iota((SUB, tokens), 0) + half * SUB
        load = mass[:, 2 + half : 3 + half] * coef
        out_ref[half * SUB : (half + 1) * SUB, :] = load + jnp.where(expert == routes, score, 0.0)


def on_device(d_out, routes, gates, slot_hidden, w_down, balance_coef):
    tokens, width = d_out.shape
    groups = lax.axis_size("expert")
    dp = lax.axis_size("dp")
    experts = groups * w_down.shape[0]
    slots, units = slot_hidden.shape[3:]
    blocks = SUB // (slots - SUB)
    part = width // blocks
    out_rows = experts * SUB
    routes_row = routes.reshape(1, tokens)
    gates_row = gates.reshape(1, tokens)
    vmem = pltpu.CompilerParams(vmem_limit_bytes=48 * 1024 * 1024)

    send, rank, mass = pl.pallas_call(
        functools.partial(pack_kernel, blocks),
        out_shape=(
            jax.ShapeDtypeStruct((out_rows, width + part), BF16),
            jax.ShapeDtypeStruct((1, tokens), jnp.int32),
            jax.ShapeDtypeStruct((SUB, 128), F32),
        ),
        compiler_params=vmem,
        name="pack",
    )(routes_row, gates_row, d_out)
    recv = lax.all_to_all(send, "expert", split_axis=0, concat_axis=0, tiled=True)
    shift = 1
    while shift < dp:
        mass = mass + lax.ppermute(mass, "dp", [(s, s ^ shift) for s in range(dp)])
        shift *= 2
    hid = jnp.transpose(slot_hidden, (0, 2, 3, 1, 4)).reshape(slots * groups, units)
    chunk = 256
    d_hid, ret = pl.pallas_call(
        functools.partial(hidden_kernel, blocks, slots),
        grid=(units // chunk,),
        in_specs=[
            pl.BlockSpec((out_rows, width + part), lambda i: (0, 0)),
            pl.BlockSpec((chunk, width), lambda i: (i, 0)),
            pl.BlockSpec((slots * groups, chunk), lambda i: (0, i)),
            pl.BlockSpec((SUB, 128), lambda i: (0, 0)),
        ],
        out_specs=(
            pl.BlockSpec((slots * groups, chunk), lambda i: (0, i)),
            pl.BlockSpec((out_rows, 128), lambda i: (0, 0)),
        ),
        out_shape=(
            jax.ShapeDtypeStruct((slots * groups, units), BF16),
            jax.ShapeDtypeStruct((out_rows, 128), F32),
        ),
        scratch_shapes=[
            pltpu.VMEM((2 * out_rows, width), BF16),
            pltpu.VMEM((out_rows, 128), F32),
        ],
        compiler_params=vmem,
        name="hidden",
    )(recv, w_down.reshape(w_down.shape[1:]), hid, mass)
    back = lax.all_to_all(ret, "expert", split_axis=0, concat_axis=0, tiled=True)
    scale = experts / (routes.shape[1] * tokens * dp * groups)
    probs = pl.pallas_call(
        functools.partial(probs_kernel, blocks, scale),
        in_specs=[pl.BlockSpec(memory_space=pltpu.SMEM)] + [pl.BlockSpec(memory_space=pltpu.VMEM)] * 4,
        out_shape=jax.ShapeDtypeStruct((experts, tokens), F32),
        compiler_params=vmem,
        name="probs",
    )(balance_coef.reshape(1, 1), routes_row, gates_row, rank, back)
    d_hidden = jnp.transpose(d_hid.reshape(1, 1, slots, groups, units), (0, 3, 1, 2, 4))
    return (probs.T, d_hidden)


def solution(mesh):
    return jax.shard_map(
        on_device,
        mesh=mesh,
        in_specs=(
            P(("dp", "expert"), None),
            P(("dp", "expert"), None),
            P(("dp", "expert"), None),
            P("dp", None, "expert", None, None),
            P("expert", None, None),
            P(),
        ),
        out_specs=(P(("dp", "expert"), None), P("dp", None, "expert", None, None)),
        check_vma=False,
    )
```

time: 301 us -> 89 us (0.30)
  blocking collectives: 169 us -> 0 us
  local copies, waits for them, and re-layouts: 58.9 us -> 2.63 us
  starting transfers between devices: 30.1 us -> 52.9 us
  matrix products: 10.9 us -> 0 us
  Pallas kernels: 0 us -> 9.76 us
  other arithmetic: 5.88 us -> 0.02 us
    psum x1 -> x0, blocking collectives: 169 us -> none  [on_device(): total_mass = lax.psum(local_mass, ('dp', 'expert'))]
    scatter x3 -> x0, local copies, waits for them, and re-layouts: 43.9 us -> none  [the longest x2 32.8 us: on_device(): jnp.zeros((expert_count, slots, width), jnp.bfloat16).at[flat, ranks]]
    ppermute x0 -> x6, starting transfers between devices: none -> 25.1 us  [on_device(): mass = mass + lax.ppermute(mass, 'dp', [(s, s ^ shift) for s in range(dp)])]
    all_to_all x3 -> x2, waiting for transfers between devices: 24.5 us -> 9.45 us  [the longest x1 7.16 us: on_device(): lax.all_to_all(ret, 'expert', split_axis=0, concat_axis=0, tiled=True)]
    ppermute x0 -> x6, waiting for transfers between devices: none -> 12.3 us  [on_device(): mass = mass + lax.ppermute(mass, 'dp', [(s, s ^ shift) for s in range(dp)])]
    dot_general x2 -> x0, matrix products: 10.9 us -> none  [the longest x1 6.26 us: on_device(): jnp.einsum('secd,efd->secf', recv_rows, w_down, preferred_element_type=jn...]
    pallas_call x0 -> x3, Pallas kernels: none -> 9.76 us  [the longest x1 6.87 us: on_device(): pl.pallas_call(functools.partial(hidden_kernel, blocks, slots), grid=(uni...]
    gather x2 -> x0, local copies, waits for them, and re-layouts: 8.23 us -> none  [the longest x1 5.76 us: on_device(): picked = back[flat, ranks]]
  transfers between devices with their start and end apart: 3 -> 8, of which waited for: 1 -> 8; matrix products, arithmetic and copies ran while one was open for 18% -> 0% of each run, Pallas kernels for 0% -> 0%
where the time goes in v1:
time: 89 us; the launch traced here: 88.5 us
  starting transfers between devices  52.9 us (59%)
  waiting for transfers between devices  21.8 us (24%)
  Pallas kernels  9.76 us (11%)
  local copies, waits for them, and re-layouts  2.63 us (3%)
  between operations  1.35 us (2%)
    ppermute x6, starting transfers between devices, on_device(): mass = mass + lax.ppermute(mass, 'dp', [(s, s ^ shift) for s in range(dp)])  25.1 us
    all_to_all x1, starting transfers between devices, on_device(): lax.all_to_all(send, 'expert', split_axis=0, concat_axis=0, tiled=True)  17.8 us
    ppermute x6, waiting for transfers between devices, on_device(): mass = mass + lax.ppermute(mass, 'dp', [(s, s ^ shift) for s in range(dp)])  12.3 us
    all_to_all x1, starting transfers between devices, on_device(): lax.all_to_all(ret, 'expert', split_axis=0, concat_axis=0, tiled=True)  10.1 us
    all_to_all x1, waiting for transfers between devices, on_device(): lax.all_to_all(ret, 'expert', split_axis=0, concat_axis=0, tiled=True)  7.16 us
    pallas_call x1, Pallas kernels, on_device(): pl.pallas_call(functools.partial(hidden_kernel, blocks, slots), grid=(uni...  6.87 us
    unnamed x12, local copies, waits for them, and re-layouts  2.63 us
    all_to_all x1, waiting for transfers between devices, on_device(): lax.all_to_all(send, 'expert', split_axis=0, concat_axis=0, tiled=True)  2.3 us
  transfers between devices with their start and end apart: 8, of which 8 were waited for; matrix products, arithmetic and copies ran while one was open for 0% of the time, Pallas kernels for 0%

profile of v1, /device:TPU:1, one launch (start us, length us, event | category | flops | bytes accessed | tf_op | source)
XLA Modules:
  0.0 88.5 jit_solution(2904809546936421777)
XLA Ops:
  0.6 0.0 copy-start
  0.6 1.3 %copy-done = bf16[128,5120]{1,0:T(8,128)(2,1)S(1)} copy-done((bf16[128,5120]{1,0:T(8,128)(2,1)S(1)}, bf16[128,5120]{1,0:T(8,128)(2,1)}, u32[]{:S(2)}) %copy-start) | copy-done | bytes 1310744
  1.9 0.0 copy-start.2
  1.9 0.7 copy-done.2
  2.6 0.0 copy-start.4
  2.6 0.7 copy-done.4
  3.3 2.2 %pack.1 = (bf16[128,6400]{1,0:T(8,128)(2,1)}, s32[1,128]{1,0:T(1,128)S(1)}, f32[8,128]{1,0:T(8,128)S(1)}) custom-call(s32[1,128]{1,0:T(1,128)S(1)} %bitcast.19, bf16[1,128]{1,0:T(2,128)(2,1)S(1)} %bitcast.21, bf16[128,5120]{1,0:T(8,128)(2,1)S(1)} %copy-done), custom_call_target="tpu_custom_call" | custom-call | tf_op jit(solution)/shard_map/pack/pallas_call | solution.py:132
  5.4 0.0 copy-start.1
  5.4 17.8 %all-to-all-start = ((bf16[16,8,6400]{2,1,0:T(8,128)(2,1)}), bf16[16,8,6400]{2,1,0:T(8,128)(2,1)S(1)}, u32[]{:S(2)}, u32[]{:S(2)}) async-start(bf16[16,8,6400]{2,1,0:T(8,128)(2,1)} %bitcast.3), calls=%async_computation | async-start | bytes 3276800 | tf_op jit(solution)/shard_map/all_to_all | solution.py:142
  23.2 1.9 %collective-permute-start = (f32[8,128]{1,0:T(8,128)S(1)}, f32[8,128]{1,0:T(8,128)S(1)}, u32[]{:S(2)}, u32[]{:S(2)}) collective-permute-start(f32[8,128]{1,0:T(8,128)S(1)} %get-tuple-element.9), channel_id=1, source_target_pairs={{0,16},{16,0},{32,48},{48,32},{64,80},{80,64},{96,112},{112,96},{1... | collective-permute-start | bytes 12296 | tf_op jit(solution)/shard_map/ppermute | solution.py:145
  25.1 2.4 %collective-permute-done = f32[8,128]{1,0:T(8,128)S(1)} collective-permute-done((f32[8,128]{1,0:T(8,128)S(1)}, f32[8,128]{1,0:T(8,128)S(1)}, u32[]{:S(2)}, u32[]{:S(2)}) %collective-permute-start) | collective-permute-done | bytes 4128 | tf_op jit(solution)/shard_map/ppermute | solution.py:145
  27.5 1.9 %collective-permute-start.1 = (f32[8,128]{1,0:T(8,128)S(1)}, f32[8,128]{1,0:T(8,128)S(1)}, u32[]{:S(2)}, u32[]{:S(2)}) collective-permute-start(f32[8,128]{1,0:T(8,128)S(1)} %add.18), channel_id=1, source_target_pairs={{0,32},{16,48},{32,0},{48,16},{64,96},{80,112},{96,64},{112,80},{1... | collective-permute-start | bytes 12296 | tf_op jit(solution)/shard_map/ppermute | solution.py:145
  29.5 3.6 %collective-permute-done.1 = f32[8,128]{1,0:T(8,128)S(1)} collective-permute-done((f32[8,128]{1,0:T(8,128)S(1)}, f32[8,128]{1,0:T(8,128)S(1)}, u32[]{:S(2)}, u32[]{:S(2)}) %collective-permute-start.1) | collective-permute-done | bytes 4128 | tf_op jit(solution)/shard_map/ppermute | solution.py:145
  33.1 7.9 %collective-permute-start.2 = (f32[8,128]{1,0:T(8,128)S(1)}, f32[8,128]{1,0:T(8,128)S(1)}, u32[]{:S(2)}, u32[]{:S(2)}) collective-permute-start(f32[8,128]{1,0:T(8,128)S(1)} %add.19), channel_id=1, source_target_pairs={{0,64},{16,80},{32,96},{48,112},{64,0},{80,16},{96,32},{112,48},{1... | collective-permute-start | bytes 12296 | tf_op jit(solution)/shard_map/ppermute | solution.py:145
  41.0 1.3 %collective-permute-done.2 = f32[8,128]{1,0:T(8,128)S(1)} collective-permute-done((f32[8,128]{1,0:T(8,128)S(1)}, f32[8,128]{1,0:T(8,128)S(1)}, u32[]{:S(2)}, u32[]{:S(2)}) %collective-permute-start.2) | collective-permute-done | bytes 4128 | tf_op jit(solution)/shard_map/ppermute | solution.py:145
  42.3 2.8 %collective-permute-start.3 = (f32[8,128]{1,0:T(8,128)S(1)}, f32[8,128]{1,0:T(8,128)S(1)}, u32[]{:S(2)}, u32[]{:S(2)}) collective-permute-start(f32[8,128]{1,0:T(8,128)S(1)} %add.20), channel_id=1, source_target_pairs={{0,128},{16,144},{32,160},{48,176},{64,192},{80,208},{96,224},{112... | collective-permute-start | bytes 12296 | tf_op jit(solution)/shard_map/ppermute | solution.py:145
  45.1 1.8 %collective-permute-done.3 = f32[8,128]{1,0:T(8,128)S(1)} collective-permute-done((f32[8,128]{1,0:T(8,128)S(1)}, f32[8,128]{1,0:T(8,128)S(1)}, u32[]{:S(2)}, u32[]{:S(2)}) %collective-permute-start.3) | collective-permute-done | bytes 4128 | tf_op jit(solution)/shard_map/ppermute | solution.py:145
  46.9 3.7 %collective-permute-start.4 = (f32[8,128]{1,0:T(8,128)S(1)}, f32[8,128]{1,0:T(8,128)S(1)}, u32[]{:S(2)}, u32[]{:S(2)}) collective-permute-start(f32[8,128]{1,0:T(8,128)S(1)} %add.21), channel_id=1, source_target_pairs={{0,256},{16,272},{32,288},{48,304},{64,320},{80,336},{96,352},{112... | collective-permute-start | bytes 12296 | tf_op jit(solution)/shard_map/ppermute | solution.py:145
  50.7 1.8 %collective-permute-done.4 = f32[8,128]{1,0:T(8,128)S(1)} collective-permute-done((f32[8,128]{1,0:T(8,128)S(1)}, f32[8,128]{1,0:T(8,128)S(1)}, u32[]{:S(2)}, u32[]{:S(2)}) %collective-permute-start.4) | collective-permute-done | bytes 4128 | tf_op jit(solution)/shard_map/ppermute | solution.py:145
  52.4 6.8 %collective-permute-start.5 = (f32[8,128]{1,0:T(8,128)S(1)}, f32[8,128]{1,0:T(8,128)S(1)}, u32[]{:S(2)}, u32[]{:S(2)}) collective-permute-start(f32[8,128]{1,0:T(8,128)S(1)} %add.22), channel_id=1, source_target_pairs={{0,512},{16,528},{32,544},{48,560},{64,576},{80,592},{96,608},{112... | collective-permute-start | bytes 12296 | tf_op jit(solution)/shard_map/ppermute | solution.py:145
  59.3 1.4 %collective-permute-done.5 = f32[8,128]{1,0:T(8,128)S(1)} collective-permute-done((f32[8,128]{1,0:T(8,128)S(1)}, f32[8,128]{1,0:T(8,128)S(1)}, u32[]{:S(2)}, u32[]{:S(2)}) %collective-permute-start.5) | collective-permute-done | bytes 4128 | tf_op jit(solution)/shard_map/ppermute | solution.py:145
  60.7 2.3 %all-to-all-done = bf16[16,8,6400]{2,1,0:T(8,128)(2,1)S(1)} async-done(((bf16[16,8,6400]{2,1,0:T(8,128)(2,1)}), bf16[16,8,6400]{2,1,0:T(8,128)(2,1)S(1)}, u32[]{:S(2)}, u32[]{:S(2)}) %all-to-all-start) | async-done | bytes 1638432 | tf_op jit(solution)/shard_map/all_to_all | solution.py:142
  63.0 0.0 copy-done.1
  63.0 0.0 copy-start.3
  63.0 0.0 copy-start.5
  63.0 6.9 %hidden.1 = (bf16[160,768]{1,0:T(8,128)(2,1)}, f32[128,128]{1,0:T(8,128)}) custom-call(bf16[128,6400]{1,0:T(8,128)(2,1)S(1)} %bitcast.16, bf16[768,5120]{1,0:T(8,128)(2,1)} %bitcast.23, bf16[160,768]{1,0:T(8,128)(2,1)S(1)} %bitcast.18, f32[8,128]{1,0:T(8,128)S(1)} %add.23.mass_ref), custom_call_target="tpu_custom_call" | custom-call | tf_op jit(solution)/shard_map/hidden/pallas_call | solution.py:149
  69.9 10.1 %all-to-all-start.1 = ((f32[16,8,128]{2,1,0:T(8,128)}), f32[16,8,128]{2,1,0:T(8,128)S(1)}, u32[]{:S(2)}, u32[]{:S(2)}) async-start(f32[16,8,128]{2,1,0:T(8,128)} %bitcast.8), calls=%async_computation.1 | async-start | bytes 131072 | tf_op jit(solution)/shard_map/all_to_all | solution.py:173
  80.6 7.2 %all-to-all-done.1 = f32[16,8,128]{2,1,0:T(8,128)S(1)} async-done(((f32[16,8,128]{2,1,0:T(8,128)}), f32[16,8,128]{2,1,0:T(8,128)S(1)}, u32[]{:S(2)}, u32[]{:S(2)}) %all-to-all-start.1) | async-done | bytes 65568 | tf_op jit(solution)/shard_map/all_to_all | solution.py:173
  87.7 0.0 copy-done.3
  87.7 0.0 copy-done.5
  87.8 0.7 probs.1
  (6 shorter events, 0.0 us)
Async XLA Ops:
  0.6 1.3 %copy-start = (bf16[128,5120]{1,0:T(8,128)(2,1)S(1)}, bf16[128,5120]{1,0:T(8,128)(2,1)}, u32[]{:S(2)}) copy-start(bf16[128,5120]{1,0:T(8,128)(2,1)} %rows_ref.1) | copy-start | bytes 3932164
  1.9 0.7 copy-start.2
  2.6 0.7 copy-start.4
  5.4 57.6 %copy-start.1 = (bf16[1,16,1,10,768]{4,1,3,2,0:T(8,128)(2,1)S(1)}, bf16[1,16,1,10,768]{4,1,3,2,0:T(8,128)(2,1)}, u32[]{:S(2)}) copy-start(bf16[1,16,1,10,768]{4,1,3,2,0:T(8,128)(2,1)} %param.9) | copy-start | bytes 737284
  5.4 57.6 %all-to-all-start = ((bf16[16,8,6400]{2,1,0:T(8,128)(2,1)}), bf16[16,8,6400]{2,1,0:T(8,128)(2,1)S(1)}, u32[]{:S(2)}, u32[]{:S(2)}) async-start(bf16[16,8,6400]{2,1,0:T(8,128)(2,1)} %bitcast.3), calls=%async_computation | async-start | bytes 3276800 | tf_op jit(solution)/shard_map/all_to_all | solution.py:142
  23.2 4.3 %collective-permute-start = (f32[8,128]{1,0:T(8,128)S(1)}, f32[8,128]{1,0:T(8,128)S(1)}, u32[]{:S(2)}, u32[]{:S(2)}) collective-permute-start(f32[8,128]{1,0:T(8,128)S(1)} %get-tuple-element.9), channel_id=1, source_target_pairs={{0,16},{16,0},{32,48},{48,32},{64,80},{80,64},{96,112},{112,96},{1... | collective-permute-start | bytes 12296 | tf_op jit(solution)/shard_map/ppermute | solution.py:145
  27.5 5.5 %collective-permute-start.1 = (f32[8,128]{1,0:T(8,128)S(1)}, f32[8,128]{1,0:T(8,128)S(1)}, u32[]{:S(2)}, u32[]{:S(2)}) collective-permute-start(f32[8,128]{1,0:T(8,128)S(1)} %add.18), channel_id=1, source_target_pairs={{0,32},{16,48},{32,0},{48,16},{64,96},{80,112},{96,64},{112,80},{1... | collective-permute-start | bytes 12296 | tf_op jit(solution)/shard_map/ppermute | solution.py:145
  33.1 9.2 %collective-permute-start.2 = (f32[8,128]{1,0:T(8,128)S(1)}, f32[8,128]{1,0:T(8,128)S(1)}, u32[]{:S(2)}, u32[]{:S(2)}) collective-permute-start(f32[8,128]{1,0:T(8,128)S(1)} %add.19), channel_id=1, source_target_pairs={{0,64},{16,80},{32,96},{48,112},{64,0},{80,16},{96,32},{112,48},{1... | collective-permute-start | bytes 12296 | tf_op jit(solution)/shard_map/ppermute | solution.py:145
  42.3 4.6 %collective-permute-start.3 = (f32[8,128]{1,0:T(8,128)S(1)}, f32[8,128]{1,0:T(8,128)S(1)}, u32[]{:S(2)}, u32[]{:S(2)}) collective-permute-start(f32[8,128]{1,0:T(8,128)S(1)} %add.20), channel_id=1, source_target_pairs={{0,128},{16,144},{32,160},{48,176},{64,192},{80,208},{96,224},{112... | collective-permute-start | bytes 12296 | tf_op jit(solution)/shard_map/ppermute | solution.py:145
  46.9 5.5 %collective-permute-start.4 = (f32[8,128]{1,0:T(8,128)S(1)}, f32[8,128]{1,0:T(8,128)S(1)}, u32[]{:S(2)}, u32[]{:S(2)}) collective-permute-start(f32[8,128]{1,0:T(8,128)S(1)} %add.21), channel_id=1, source_target_pairs={{0,256},{16,272},{32,288},{48,304},{64,320},{80,336},{96,352},{112... | collective-permute-start | bytes 12296 | tf_op jit(solution)/shard_map/ppermute | solution.py:145
  52.4 8.2 %collective-permute-start.5 = (f32[8,128]{1,0:T(8,128)S(1)}, f32[8,128]{1,0:T(8,128)S(1)}, u32[]{:S(2)}, u32[]{:S(2)}) collective-permute-start(f32[8,128]{1,0:T(8,128)S(1)} %add.22), channel_id=1, source_target_pairs={{0,512},{16,528},{32,544},{48,560},{64,576},{80,592},{96,608},{112... | collective-permute-start | bytes 12296 | tf_op jit(solution)/shard_map/ppermute | solution.py:145
  63.0 24.8 %copy-start.3 = (s32[128,1]{0,1:T(1,128)S(1)}, s32[128,1]{0,1:T(1,128)}, u32[]{:S(2)}) copy-start(s32[128,1]{0,1:T(1,128)} %param.7) | copy-start | bytes 1540
  63.0 24.8 %copy-start.5 = (bf16[128,1]{0,1:T(2,128)(2,1)S(1)}, bf16[128,1]{0,1:T(2,128)(2,1)}, u32[]{:S(2)}) copy-start(bf16[128,1]{0,1:T(2,128)(2,1)} %param.8) | copy-start | bytes 772
  69.9 17.9 %all-to-all-start.1 = ((f32[16,8,128]{2,1,0:T(8,128)}), f32[16,8,128]{2,1,0:T(8,128)S(1)}, u32[]{:S(2)}, u32[]{:S(2)}) async-start(f32[16,8,128]{2,1,0:T(8,128)} %bitcast.8), calls=%async_computation.1 | async-start | bytes 131072 | tf_op jit(solution)/shard_map/all_to_all | solution.py:173
